TPU v7x, 32 devices: a whole 2x2x4 slice. The times are simulated.
32 devices in a mesh: wide: 8 (over y, x, core), narrow: 4 (over z).
Axes of the slice: x: 2, y: 2, z: 4, core: 2. Of those that a mesh axis runs over, the one named last changes fastest.
Arguments:
- x_zero: bfloat16 [4608, 3456], P(('wide', 'narrow')), may hold values from -6 to 6
- labels: int32 [4608], P(('wide', 'narrow')), may hold values 0 or 1
- cross_u: bfloat16 [3456, 256], replicated, may hold values from -0.375 to 0.375
- cross_v: bfloat16 [3456, 256], replicated, may hold values from -0.109375 to 0.109375
- cross_bias: float32 [3456], replicated, may hold values from -3 to 3
- head: float32 [3456], replicated, may hold values from -0.109375 to 0.109375
- hot_table: float32 [8192, 128], replicated, may hold values from -6 to 6
- hot_acc: float32 [8192], replicated, may hold values from 0.01 to 100
- cold_table: float32 [65536, 128], P(('wide', 'narrow')), may hold values from -6 to 6
- cold_acc: float32 [65536], P(('wide', 'narrow')), may hold values from 0.0001 to 0.01
- hot_ids: int32 [4608, 26, 19], P(('wide', 'narrow')), may hold values from 0 to 8191
- cold_owner: int32 [4608, 26, 1], P(('wide', 'narrow')), may hold values from 0 to 31; in each aligned block of 3744 rows (0 to 3743, 3744 to 7487, ..., all dimensions but the last counted through in order) at most 468 rows name the same one
- cold_slot: int32 [4608, 26], P(('wide', 'narrow')), may hold values from 0 to 2047
Outputs:
- hot_out: float32 [8192, 128], replicated
- cold_out: float32 [65536, 128], P(('wide', 'narrow'))
- grad_u: bfloat16 [3456, 256], replicated
- grad_v: bfloat16 [3456, 256], replicated
- grad_bias: float32 [3456], replicated
Inputs may be any that keep to these rules, and one draw needn't show every extreme that they name: `cold_owner`: an owner is a device's index over wide and narrow, wide slowest. Among the 3744 bags of one device no owner is named by more than 468 bags, a bound that some block reaches.
All inputs are finite; a program needn't handle non-finite values. No bound on the sum of `labels` on one device may be relied on, other than what follows from the above.
Results may differ from a plain program's by a relative error of at most 0.0058.
Values may be sent and summed in bfloat16 or wider, within the bound.
A program may use at most 128 MiB of HBM per device.

v0:
```python
import math

import jax
import jax.numpy as jnp
from jax import lax
from jax.sharding import PartitionSpec as P

LEARN_RATE = 0.5
EPSILON = 1e-08


def adagrad_rows(table, accum, grad):
    new_acc = accum + jnp.mean(grad * grad, axis=1)
    return table - LEARN_RATE * grad / (jnp.sqrt(new_acc)[:, None] + EPSILON)


def per_device(
    x_zero,
    labels,
    cross_u,
    cross_v,
    cross_bias,
    head,
    hot_table,
    hot_acc,
    cold_table,
    cold_acc,
    hot_ids,
    cold_owner,
    cold_slot,
):
    samples = x_zero.shape[0]
    emb_width = cold_table.shape[1]
    features = hot_ids.shape[1]
    lanes = hot_ids.shape[2]
    shard_rows = cold_table.shape[0]
    hot_rows_all = hot_table.shape[0]
    bag_count = samples * features
    proj_b = jnp.dot(x_zero, cross_v, preferred_element_type=jnp.float32).astype(jnp.bfloat16)
    mixed = jnp.dot(proj_b, cross_u.T, preferred_element_type=jnp.float32)
    scale = mixed + cross_bias[None, :]
    x_float = x_zero.astype(jnp.float32)
    crossed = x_float * scale + x_float
    logit = jnp.sum(crossed * head[None, :], axis=1)
    delta = jax.nn.sigmoid(logit) - labels.astype(jnp.float32)
    upstream = delta[:, None] * head[None, :]
    dscale = upstream * x_float
    dscale_b = dscale.astype(jnp.bfloat16)
    dproj_b = jnp.dot(dscale_b, cross_u, preferred_element_type=jnp.float32).astype(jnp.bfloat16)
    pooled = upstream[:, emb_width:] * (scale[:, emb_width:] + 1.0) + jnp.dot(
        dproj_b, cross_v[emb_width:].T, preferred_element_type=jnp.float32
    )
    flat_b = pooled.astype(jnp.bfloat16).reshape(bag_count, emb_width)
    owners = cold_owner.reshape(bag_count)
    places = cold_slot.reshape(bag_count)
    devices = lax.axis_size(("wide", "narrow"))
    capacity = 4 * bag_count // devices
    order = jnp.argsort(owners, stable=True)
    sorted_owner = owners[order]
    counts = jnp.sum(
        (owners[:, None] == jnp.arange(devices, dtype=jnp.int32)[None, :]).astype(jnp.int32), axis=0
    )
    starts = jnp.cumsum(counts) - counts
    position = jnp.arange(bag_count, dtype=jnp.int32) - starts[sorted_owner]
    target = sorted_owner * capacity + position
    send_grad = (
        jnp.zeros((devices * capacity, emb_width), jnp.bfloat16).at[target].set(flat_b[order])
    )
    send_place = jnp.zeros((devices * capacity,), jnp.int32).at[target].set(places[order])
    recv_grad, recv_place = (
        lax.all_to_all(
            send_grad.reshape(devices, capacity, emb_width),
            ("wide", "narrow"),
            split_axis=0,
            concat_axis=0,
            tiled=True,
        ),
        lax.all_to_all(
            send_place.reshape(devices, capacity),
            ("wide", "narrow"),
            split_axis=0,
            concat_axis=0,
            tiled=True,
        ),
    )
    recv_rows = recv_grad.reshape(-1, emb_width)
    recv_where = recv_place.reshape(-1)
    slot_block = math.gcd(shard_rows, 512)

    def cold_block(first):
        columns = first + jnp.arange(slot_block, dtype=jnp.int32)
        onehot = (recv_where[:, None] == columns[None, :]).astype(jnp.bfloat16)
        return lax.dot_general(
            onehot, recv_rows, (((0,), (0,)), ((), ())), preferred_element_type=jnp.float32
        )

    cold_firsts = jnp.arange(0, shard_rows, slot_block, dtype=jnp.int32)
    cold_grad = lax.map(cold_block, cold_firsts).reshape(shard_rows, emb_width)
    cold_out = adagrad_rows(cold_table, cold_acc, cold_grad)
    flat_ids = hot_ids.reshape(bag_count, lanes)
    hot_block = math.gcd(hot_rows_all, 1024)

    def hot_part(first):
        columns = first + jnp.arange(hot_block, dtype=jnp.int32)
        tally = jnp.zeros((bag_count, hot_block), jnp.bfloat16)
        for lane in range(lanes):
            tally = tally + (flat_ids[:, lane][:, None] == columns[None, :]).astype(jnp.bfloat16)
        return lax.dot_general(
            tally, flat_b, (((0,), (0,)), ((), ())), preferred_element_type=jnp.float32
        )

    hot_firsts = jnp.arange(0, hot_rows_all, hot_block, dtype=jnp.int32)
    hot_local = lax.map(hot_part, hot_firsts).reshape(hot_rows_all, emb_width)
    part_u = lax.dot_general(
        dscale_b, proj_b, (((0,), (0,)), ((), ())), preferred_element_type=jnp.float32
    )
    part_v = lax.dot_general(
        x_zero, dproj_b, (((0,), (0,)), ((), ())), preferred_element_type=jnp.float32
    )
    part_c = jnp.sum(dscale, axis=0)
    hot_grad, sum_u, sum_v, sum_c = lax.psum(
        (hot_local, part_u, part_v, part_c), ("wide", "narrow")
    )
    hot_out = adagrad_rows(hot_table, hot_acc, hot_grad)
    return (hot_out, cold_out, sum_u.astype(jnp.bfloat16), sum_v.astype(jnp.bfloat16), sum_c)


def solution(mesh):
    placed = (
        P(("wide", "narrow"), None),
        P(("wide", "narrow")),
        P(),
        P(),
        P(),
        P(),
        P(),
        P(),
        P(("wide", "narrow"), None),
        P(("wide", "narrow")),
        P(("wide", "narrow"), None, None),
        P(("wide", "narrow"), None, None),
        P(("wide", "narrow"), None),
    )
    return jax.shard_map(
        per_device,
        mesh=mesh,
        in_specs=placed,
        out_specs=(P(), P(("wide", "narrow"), None), P(), P(), P()),
        check_vma=False,
    )
```

profile of v0, /device:TPU:24, one launch (start us, length us, event | category | flops | bytes accessed | tf_op | source)
XLA Modules:
  0.0 669.0 jit_solution(11999604817901376762)
XLA Ops:
  10.2 5.8 sort.17
  16.0 19.9 %gather_fusion = s32[3744]{0:T(1024)S(1)} fusion(s32[3744]{0:T(1024)S(1)} %reshape.130, s32[4096]{0:T(1024)S(1)} %pad_clamp_fusion), kind=kCustom, calls=%fused_computation | custom fusion | bytes 44928 | tf_op jit(solution)/shard_map/gather | solution.py:59
  36.2 19.9 %gather_fusion.1 = s32[3744]{0:T(1024)S(1)} fusion(s32[3744]{0:T(1024)S(1)} %reshape.133, s32[4096]{0:T(1024)S(1)} %pad_clamp_fusion), kind=kCustom, calls=%fused_computation.1 | custom fusion | bytes 44928 | tf_op jit(solution)/shard_map/gather | solution.py:69
  61.6 15.8 %select_select_fusion = s32[3744]{0:T(1024)S(1)} fusion(pred[3744]{0:T(1024)(128)(4,1)S(1)} %get-tuple-element.126, pred[3744]{0:T(1024)(128)(4,1)S(1)} %get-tuple-element.125, pred[3744]{0:T(1024)(128)(4,1)S(1)} %get-tuple-element.124, pred[3744]{0:T(1024)(128)(4,1)S(1)} %get-tuple-element.123, pred[3744]{0:T(1024)(128)(4,1)S(1)} %get-tuple-element.122, ...), kind=kLoop, calls=%fused_computation.158 | loop fusion | flops 93600 | bytes 123652 | tf_op jit(solution)/shard_map/gather | solution.py:64
  77.5 18.2 %scatter_custom_fusion = s32[14976]{0:T(1024)S(1)} fusion(s32[3744]{0:T(1024)S(1)} %fusion.72, s32[3744]{0:T(1024)S(1)} %gather_fusion.1, s32[]{:T(128)} %copy.60), kind=kCustom, calls=%fused_computation.155 | custom fusion | bytes 59908 | tf_op jit(solution)/shard_map/scatter | solution.py:69
  96.5 6.3 all-to-all-start
  113.5 30.2 %scatter_custom_fusion.1 = bf16[14976,128]{1,0:T(8,128)(2,1)} fusion(s32[3744]{0:T(1024)} %copy-done.17, bf16[]{:T(256)} %constant.18.clone.1, bf16[3744,128]{1,0:T(8,128)(2,1)S(1)} %reshape.128, s32[4096]{0:T(1024)S(1)} %pad_clamp_fusion), kind=kCustom, calls=%fused_computation.103 | custom fusion | bytes 3834368 | tf_op jit(solution)/shard_map/scatter | solution.py:67
  143.7 5.8 reshape.134
  149.5 5.9 all-to-all-start.1
  155.6 267.2 %while.21 = (s32[]{:T(128)}, f32[8,1024,128]{2,1,0:T(8,128)}, s32[3744,19]{0,1:T(8,128)S(1)}, s32[8]{0:T(128)S(1)}, bf16[3744,128]{1,0:T(8,128)(2,1)S(1)}, /*index=5*/s32[]{:T(128)}) while((s32[]{:T(128)}, f32[8,1024,128]{2,1,0:T(8,128)}, s32[3744,19]{0,1:T(8,128)S(1)}, s32[8]{0:T(128)S(1)}, bf16[3744,128]{1,0:T(8,128)(2,1)S(1)}, ...), condition=%wide.region_2.3_spmd, body=%wide.region_1.0_spmd.sunk | while | flops 1196164096 | bytes 2344673 | solution.py:113
  157.6 31.4 %fusion.100 = f32[8,1024,128]{2,1,0:T(8,128)} fusion(f32[8,1024,128]{2,1,0:T(8,128)} %get-tuple-element.323, s32[]{:T(128)S(6)} %copy.44, bf16[3744,128]{1,0:T(8,128)(2,1)S(1)} %get-tuple-element.332, s32[1024]{0:T(1024)S(1)} %iota_add_fusion.5, s32[3744]{0:T(1024)S(1)} %get-tuple-element.291, s32[3744]{0:T(1024)S(1)} %get-tuple-element.292, ...), kind=kOutput, calls=%fused_computation.70.clone.2 | convolution fusion | flops 1196163072 | bytes 1771396 | tf_op jit(solution)/shard_map/while/body/eval_jaxpr/dot_general | solution.py:108
  191.1 31.4 %fusion.100 = f32[8,1024,128]{2,1,0:T(8,128)} fusion(f32[8,1024,128]{2,1,0:T(8,128)} %get-tuple-element.323, s32[]{:T(128)S(6)} %copy.44, bf16[3744,128]{1,0:T(8,128)(2,1)S(1)} %get-tuple-element.332, s32[1024]{0:T(1024)S(1)} %iota_add_fusion.5, s32[3744]{0:T(1024)S(1)} %get-tuple-element.291, s32[3744]{0:T(1024)S(1)} %get-tuple-element.292, ...), kind=kOutput, calls=%fused_computation.70.clone.2 | convolution fusion | flops 1196163072 | bytes 1771396 | tf_op jit(solution)/shard_map/while/body/eval_jaxpr/dot_general | solution.py:108
  224.5 31.4 %fusion.100 = f32[8,1024,128]{2,1,0:T(8,128)} fusion(f32[8,1024,128]{2,1,0:T(8,128)} %get-tuple-element.323, s32[]{:T(128)S(6)} %copy.44, bf16[3744,128]{1,0:T(8,128)(2,1)S(1)} %get-tuple-element.332, s32[1024]{0:T(1024)S(1)} %iota_add_fusion.5, s32[3744]{0:T(1024)S(1)} %get-tuple-element.291, s32[3744]{0:T(1024)S(1)} %get-tuple-element.292, ...), kind=kOutput, calls=%fused_computation.70.clone.2 | convolution fusion | flops 1196163072 | bytes 1771396 | tf_op jit(solution)/shard_map/while/body/eval_jaxpr/dot_general | solution.py:108
  257.9 31.4 %fusion.100 = f32[8,1024,128]{2,1,0:T(8,128)} fusion(f32[8,1024,128]{2,1,0:T(8,128)} %get-tuple-element.323, s32[]{:T(128)S(6)} %copy.44, bf16[3744,128]{1,0:T(8,128)(2,1)S(1)} %get-tuple-element.332, s32[1024]{0:T(1024)S(1)} %iota_add_fusion.5, s32[3744]{0:T(1024)S(1)} %get-tuple-element.291, s32[3744]{0:T(1024)S(1)} %get-tuple-element.292, ...), kind=kOutput, calls=%fused_computation.70.clone.2 | convolution fusion | flops 1196163072 | bytes 1771396 | tf_op jit(solution)/shard_map/while/body/eval_jaxpr/dot_general | solution.py:108
  291.3 31.4 %fusion.100 = f32[8,1024,128]{2,1,0:T(8,128)} fusion(f32[8,1024,128]{2,1,0:T(8,128)} %get-tuple-element.323, s32[]{:T(128)S(6)} %copy.44, bf16[3744,128]{1,0:T(8,128)(2,1)S(1)} %get-tuple-element.332, s32[1024]{0:T(1024)S(1)} %iota_add_fusion.5, s32[3744]{0:T(1024)S(1)} %get-tuple-element.291, s32[3744]{0:T(1024)S(1)} %get-tuple-element.292, ...), kind=kOutput, calls=%fused_computation.70.clone.2 | convolution fusion | flops 1196163072 | bytes 1771396 | tf_op jit(solution)/shard_map/while/body/eval_jaxpr/dot_general | solution.py:108
  324.7 31.4 %fusion.100 = f32[8,1024,128]{2,1,0:T(8,128)} fusion(f32[8,1024,128]{2,1,0:T(8,128)} %get-tuple-element.323, s32[]{:T(128)S(6)} %copy.44, bf16[3744,128]{1,0:T(8,128)(2,1)S(1)} %get-tuple-element.332, s32[1024]{0:T(1024)S(1)} %iota_add_fusion.5, s32[3744]{0:T(1024)S(1)} %get-tuple-element.291, s32[3744]{0:T(1024)S(1)} %get-tuple-element.292, ...), kind=kOutput, calls=%fused_computation.70.clone.2 | convolution fusion | flops 1196163072 | bytes 1771396 | tf_op jit(solution)/shard_map/while/body/eval_jaxpr/dot_general | solution.py:108
  358.1 31.4 %fusion.100 = f32[8,1024,128]{2,1,0:T(8,128)} fusion(f32[8,1024,128]{2,1,0:T(8,128)} %get-tuple-element.323, s32[]{:T(128)S(6)} %copy.44, bf16[3744,128]{1,0:T(8,128)(2,1)S(1)} %get-tuple-element.332, s32[1024]{0:T(1024)S(1)} %iota_add_fusion.5, s32[3744]{0:T(1024)S(1)} %get-tuple-element.291, s32[3744]{0:T(1024)S(1)} %get-tuple-element.292, ...), kind=kOutput, calls=%fused_computation.70.clone.2 | convolution fusion | flops 1196163072 | bytes 1771396 | tf_op jit(solution)/shard_map/while/body/eval_jaxpr/dot_general | solution.py:108
  391.5 31.4 %fusion.100 = f32[8,1024,128]{2,1,0:T(8,128)} fusion(f32[8,1024,128]{2,1,0:T(8,128)} %get-tuple-element.323, s32[]{:T(128)S(6)} %copy.44, bf16[3744,128]{1,0:T(8,128)(2,1)S(1)} %get-tuple-element.332, s32[1024]{0:T(1024)S(1)} %iota_add_fusion.5, s32[3744]{0:T(1024)S(1)} %get-tuple-element.291, s32[3744]{0:T(1024)S(1)} %get-tuple-element.292, ...), kind=kOutput, calls=%fused_computation.70.clone.2 | convolution fusion | flops 1196163072 | bytes 1771396 | tf_op jit(solution)/shard_map/while/body/eval_jaxpr/dot_general | solution.py:108
  429.1 156.4 %all-reduce.5 = (bf16[3456,256]{1,0:T(8,128)(2,1)}, bf16[3456,256]{0,1:T(8,128)(2,1)S(1)}, f32[3456]{0:T(1024)}) all-reduce(f32[3456,256]{1,0:T(8,128)} %fusion.66, f32[3456,256]{0,1:T(8,128)} %convolution_bitcast_fusion, f32[3456]{0:T(1024)S(1)} %copy-done.13), channel_id=1, replica_groups=mesh['wide'=8,'narrow'=4] {'wide','narrow'}, use_global_device_ids=true, to_apply=%region_13.14 | all-reduce | flops 1772928 | bytes 10644480 | tf_op jit(solution)/shard_map/psum | solution.py:121
  602.4 56.4 %while.22 = (s32[]{:T(128)}, f32[4,512,128]{2,1,0:T(8,128)}, s32[32,468]{1,0:T(8,128)}, s32[4]{0:T(128)S(1)}, bf16[14976,128]{1,0:T(8,128)(2,1)}, /*index=5*/s32[14976]{0:T(1024)S(1)}, s32[]{:T(128)}) while((s32[]{:T(128)}, f32[4,512,128]{2,1,0:T(8,128)}, s32[32,468]{1,0:T(8,128)}, s32[4]{0:T(128)S(1)}, ...), condition=%wide.wide.region_11.12_spmd, body=%wide.wide.region_10.11_spmd.sunk | while | flops 1970602496 | bytes 4160105 | solution.py:98
  603.7 12.9 %fusion.103 = f32[4,512,128]{2,1,0:T(8,128)} fusion(f32[4,512,128]{2,1,0:T(8,128)} %get-tuple-element.342, s32[]{:T(128)S(6)} %copy.51, bf16[14976,128]{1,0:T(8,128)(2,1)} %get-tuple-element.352, s32[512]{0:T(512)S(1)} %iota_add_fusion.6, s32[14976]{0:T(1024)S(1)} %get-tuple-element.353), kind=kOutput, calls=%fused_computation.10.clone.clone.1 | convolution fusion | flops 1970601984 | bytes 4157956 | tf_op jit(solution)/shard_map/while/body/eval_jaxpr/dot_general | solution.py:93
  617.8 12.9 %fusion.103 = f32[4,512,128]{2,1,0:T(8,128)} fusion(f32[4,512,128]{2,1,0:T(8,128)} %get-tuple-element.342, s32[]{:T(128)S(6)} %copy.51, bf16[14976,128]{1,0:T(8,128)(2,1)} %get-tuple-element.352, s32[512]{0:T(512)S(1)} %iota_add_fusion.6, s32[14976]{0:T(1024)S(1)} %get-tuple-element.353), kind=kOutput, calls=%fused_computation.10.clone.clone.1 | convolution fusion | flops 1970601984 | bytes 4157956 | tf_op jit(solution)/shard_map/while/body/eval_jaxpr/dot_general | solution.py:93
  631.8 12.9 %fusion.103 = f32[4,512,128]{2,1,0:T(8,128)} fusion(f32[4,512,128]{2,1,0:T(8,128)} %get-tuple-element.342, s32[]{:T(128)S(6)} %copy.51, bf16[14976,128]{1,0:T(8,128)(2,1)} %get-tuple-element.352, s32[512]{0:T(512)S(1)} %iota_add_fusion.6, s32[14976]{0:T(1024)S(1)} %get-tuple-element.353), kind=kOutput, calls=%fused_computation.10.clone.clone.1 | convolution fusion | flops 1970601984 | bytes 4157956 | tf_op jit(solution)/shard_map/while/body/eval_jaxpr/dot_general | solution.py:93
  645.9 12.9 %fusion.103 = f32[4,512,128]{2,1,0:T(8,128)} fusion(f32[4,512,128]{2,1,0:T(8,128)} %get-tuple-element.342, s32[]{:T(128)S(6)} %copy.51, bf16[14976,128]{1,0:T(8,128)(2,1)} %get-tuple-element.352, s32[512]{0:T(512)S(1)} %iota_add_fusion.6, s32[14976]{0:T(1024)S(1)} %get-tuple-element.353), kind=kOutput, calls=%fused_computation.10.clone.clone.1 | convolution fusion | flops 1970601984 | bytes 4157956 | tf_op jit(solution)/shard_map/while/body/eval_jaxpr/dot_general | solution.py:93
  (126 shorter events, 66.8 us)
Async XLA Ops:
  7.2 97.5 %copy-start = (bf16[3456,256]{1,0:T(8,128)(2,1)S(1)}, bf16[3456,256]{1,0:T(8,128)(2,1)}, u32[]{:S(2)}) copy-start(bf16[3456,256]{1,0:T(8,128)(2,1)} %param.19) | copy-start | bytes 5308420
  16.0 19.9 %copy-start.15 = (s32[144,26]{0,1:T(8,128)S(1)}, s32[144,26]{0,1:T(8,128)}, u32[]{:S(2)}) copy-start(s32[144,26]{0,1:T(8,128)} %param.29) | copy-start | bytes 44932
  36.2 66.6 %copy-start.1 = (bf16[144,3456]{1,0:T(8,128)(2,1)S(1)}, bf16[144,3456]{1,0:T(8,128)(2,1)}, u32[]{:S(2)}) copy-start(bf16[144,3456]{1,0:T(8,128)(2,1)} %param.17) | copy-start | bytes 2985988
  36.2 68.6 %copy-start.11 = (f32[3456]{0:T(1024)S(1)}, f32[3456]{0:T(1024)}, u32[]{:S(2)}) copy-start(f32[3456]{0:T(1024)} %param.22) | copy-start | bytes 41476
  36.2 68.5 %copy-start.16 = (f32[3456]{0:T(1024)S(1)}, f32[3456]{0:T(1024)}, u32[]{:S(2)}) copy-start(f32[3456]{0:T(1024)} %param.21) | copy-start | bytes 41476
  77.5 28.2 %copy-start.17 = (s32[3744]{0:T(1024)}, s32[3744]{0:T(1024)S(1)}, u32[]{:S(2)}) copy-start(s32[3744]{0:T(1024)S(1)} %fusion.72) | copy-start | bytes 44932
  96.5 53.0 %all-to-all-start = ((s32[32,1,468]{2,1,0:T(1,128)}), s32[32,1,468]{2,1,0:T(1,128)}, u32[]{:S(2)}, u32[]{:S(2)}) async-start(s32[32,1,468]{2,1,0:T(1,128)} %all_to_all.11), calls=%async_computation | async-start | bytes 131072 | tf_op jit(solution)/shard_map/all_to_all | solution.py:78
  102.8 2.9 copy-start.21
  104.7 1.5 copy-start.6
  105.7 1.5 copy-start.4
  105.7 3.2 copy-start.18
  149.5 447.1 %all-to-all-start.1 = ((bf16[32,468,128]{2,1,0:T(8,128)(2,1)}), bf16[32,468,128]{2,1,0:T(8,128)(2,1)}, u32[]{:S(2)}, u32[]{:S(2)}) async-start(bf16[32,468,128]{2,1,0:T(8,128)(2,1)} %reshape.134), calls=%async_computation.1 | async-start | bytes 7733248 | tf_op jit(solution)/shard_map/all_to_all | solution.py:71
  155.4 433.4 %all-reduce.4.cloned.1.call-start = ((), (), s32[]{:S(2)}) async-start(), calls=%async_computation.2 | async-start | bytes 8388608 | tf_op jit(solution)/shard_map/psum | solution.py:121
  422.9 1.2 copy-start.2
  422.9 1.2 copy-start.7
  422.9 1.2 copy-start.12
  422.9 1.2 copy-start.19
  422.9 3.8 copy-start.9
  424.1 5.1 copy-start.13
  587.7 4.5 copy-start.14
  588.6 7.9 %copy-start.10 = (s32[32,1,468]{2,0,1:T(8,128)}, s32[32,1,468]{2,0,1:T(8,128)S(1)}, u32[]{:S(2)}) copy-start(s32[32,1,468]{2,0,1:T(8,128)S(1)} %copy.39) | copy-start | bytes 179716
  588.8 3.5 copy-start.3
  602.4 58.0 %copy-start.20 = (f32[2048]{0:T(1024)S(1)}, f32[2048]{0:T(1024)}, u32[]{:S(2)}) copy-start(f32[2048]{0:T(1024)} %param.26) | copy-start | bytes 24580
  602.4 58.0 %copy-start.5 = (f32[2048,128]{1,0:T(8,128)S(1)}, f32[2048,128]{1,0:T(8,128)}, u32[]{:S(2)}) copy-start(f32[2048,128]{1,0:T(8,128)} %param.25) | copy-start | bytes 3145732
  (1 other events, 1.0 us)
Sparse Core Ops, SparseCore 0:
  423.0 149.7 all-reduce.3
where the time goes:
time: 677 us; the launch traced here: 669 us
  matrix products  313 us (46%)
  blocking collectives  156 us (23%)
  local copies, waits for them, and re-layouts  125 us (18%)
  other arithmetic  46.6 us (7%)
  between operations  14.9 us (2%)
  starting transfers between devices  12.4 us (2%)
    dot_general x8, matrix products, hot_part(): lax.dot_general(tally, flat_b, (((0,), (0,)), ((), ())), preferred_elemen...  251 us
    psum x1, blocking collectives, per_device(): lax.psum((hot_local, part_u, part_v, part_c), ('wide', 'narrow'))  156 us
    dot_general x4, matrix products, cold_block(): lax.dot_general(onehot, recv_rows, (((0,), (0,)), ((), ())), preferred_el...  51.6 us
    scatter x1, local copies, waits for them, and re-layouts, per_device(): jnp.zeros((devices * capacity, emb_width), jnp.bfloat16).at[target]  30.2 us
    gather x3, other arithmetic, per_device(): position = jnp.arange(bag_count, dtype=jnp.int32) - starts[sorted_owner]  21.3 us
    gather x1, local copies, waits for them, and re-layouts, per_device(): sorted_owner = owners[order]  19.9 us
    gather x1, local copies, waits for them, and re-layouts, per_device(): places[order]  19.9 us
    scatter x1, local copies, waits for them, and re-layouts, per_device(): jnp.zeros((devices * capacity,), jnp.int32).at[target].set(places[order])  18.2 us
  transfers between devices with their start and end apart: 3, of which 0 were waited for; matrix products, arithmetic and copies ran while one was open for 49% of the time, Pallas kernels for 0%

commit v1 on v0

v1 whole, which is shorter than its diff:
```python
import functools

import jax
import jax.numpy as jnp
from jax import lax
from jax.experimental import pallas as pl
from jax.experimental.pallas import tpu as pltpu
from jax.sharding import PartitionSpec as P

LEARN_RATE = 0.5
EPSILON = 1e-08
AXES = ("wide", "narrow")
NT = (((1,), (1,)), ((), ()))
TN = (((0,), (0,)), ((), ()))
GROUP = 4
UNROLL = 8
COLD_WAYS = 4
HOT_WAYS = 8


def list_kernel(samples, features, stride, row_bits, shard_rows, owner_ref, slot_ref, me_ref, out_ref, count_ref):
    devices = count_ref.shape[0]

    @pl.loop(0, devices)
    def _(o):
        count_ref[o] = 0

    offset = me_ref[0] * samples

    @pl.loop(0, samples)
    def _(s):
        for f in range(features):
            b = s * features + f
            o = owner_ref[b]
            c = count_ref[o]
            out_ref[o * stride + c] = (slot_ref[b] << row_bits) + (offset + (f * GROUP * samples) + s)
            count_ref[o] = c + 1

    @pl.loop(0, devices)
    def _(o):
        c = count_ref[o]
        for i in range(UNROLL - 1):
            out_ref[o * stride + c + i] = shard_rows << row_bits
        out_ref[o * stride + (stride - 1)] = c


def hot_kernel(samples, features, lanes, ids_ref, g_ref, out_ref, *accs):
    rows, width = out_ref.shape
    step = 128

    @pl.loop(0, rows // step)
    def _(i):
        for acc in accs:
            acc[pl.ds(i * step, step), :] = jnp.zeros((step, width), jnp.float32)

    @pl.loop(0, samples)
    def _(s):
        @pl.loop(0, features, unroll=2)
        def _(f):
            row = g_ref[pl.ds(f * samples + s, 1), :]
            base = (s * features + f) * lanes
            for j in range(lanes):
                acc = accs[j % len(accs)]
                i = ids_ref[base + j]
                acc[pl.ds(i, 1), :] = acc[pl.ds(i, 1), :] + row

    @pl.loop(0, rows // step)
    def _(i):
        total = accs[0][pl.ds(i * step, step), :]
        for acc in accs[1:]:
            total = total + acc[pl.ds(i * step, step), :]
        out_ref[pl.ds(i * step, step), :] = total.astype(out_ref.dtype)


def cold_kernel(
    stride, row_bits, lists_ref, pd_ref, delta_ref, u_ref, v_ref, bias_ref, head_ref, table_ref, acc_ref, after_ref,
    out_ref, rows_ref, *accs
):
    step = pl.program_id(0)
    shard_rows, width = out_ref.shape
    rank = u_ref.shape[2]
    pairs, wide = u_ref.shape[0], u_ref.shape[1]
    block = pd_ref.shape[0]

    @pl.when(step == 0)
    def _():
        for acc in accs:
            acc[...] = jnp.zeros_like(acc)

    @pl.loop(0, pairs)
    def _(p):
        scale = lax.dot_general(pd_ref[:, :rank], u_ref[p], NT, preferred_element_type=jnp.float32) + bias_ref[p]
        back = lax.dot_general(pd_ref[:, rank:], v_ref[p], NT, preferred_element_type=jnp.float32)
        pooled = (delta_ref[...] * head_ref[p]) * (scale + 1.0) + back
        pooled = pooled.astype(jnp.bfloat16).astype(jnp.float32)
        for h in range(wide // width):
            first = pl.multiple_of((p * (wide // width) + h) * block, 8)
            rows_ref[pl.ds(first, block), :] = pooled[:, h * width:(h + 1) * width]

    for k in range(GROUP):
        count = lists_ref[0, 0, k * stride + (stride - 1)]

        @pl.loop(0, (count + (UNROLL - 1)) // UNROLL)
        def _(i):
            entries = [lists_ref[0, 0, k * stride + i * UNROLL + n] for n in range(UNROLL)]
            values = [rows_ref[pl.ds(e & ((1 << row_bits) - 1), 1), :] for e in entries]
            for n in range(UNROLL):
                acc = accs[n % len(accs)]
                slot = entries[n] >> row_bits
                acc[pl.ds(slot, 1), :] = acc[pl.ds(slot, 1), :] + values[n]

    @pl.when(step == pl.num_programs(0) - 1)
    def _():
        part = 256

        @pl.loop(0, shard_rows // part)
        def _(i):
            here = pl.ds(pl.multiple_of(i * part, part), part)
            grad = accs[0][here, :]
            for acc in accs[1:]:
                grad = grad + acc[here, :]
            new_acc = acc_ref[here, :] + jnp.mean(grad * grad, axis=1, keepdims=True)
            out_ref[here, :] = table_ref[here, :] - LEARN_RATE * grad / (jnp.sqrt(new_acc) + EPSILON)


def per_device(
    x_zero, labels, cross_u, cross_v, cross_bias, head, hot_table, hot_acc,
    cold_table, cold_acc, hot_ids, cold_owner, cold_slot,
):
    samples, depth = x_zero.shape
    shard_rows, width = cold_table.shape
    features, lanes = hot_ids.shape[1:]
    hot_rows = hot_table.shape[0]
    rank = cross_u.shape[1]
    bags = samples * features
    devices = lax.axis_size(AXES)
    capacity = 4 * bags // devices
    stride = -(-(capacity + UNROLL) // 128) * 128
    row_bits = (GROUP * bags - 1).bit_length()
    me = lax.axis_index(AXES)

    lists = pl.pallas_call(
        functools.partial(list_kernel, samples, features, stride, row_bits, shard_rows),
        out_shape=jax.ShapeDtypeStruct((devices * stride,), jnp.int32),
        in_specs=[pl.BlockSpec(memory_space=pltpu.SMEM)] * 3,
        out_specs=pl.BlockSpec(memory_space=pltpu.SMEM),
        scratch_shapes=[pltpu.SMEM((devices,), jnp.int32)],
        name="list_bags",
    )(cold_owner.reshape(bags), cold_slot.reshape(bags), lax.rem(me, GROUP).astype(jnp.int32).reshape(1))
    lists = lax.all_to_all(lists.reshape(devices, stride), AXES, split_axis=0, concat_axis=0, tiled=True)

    proj_b = jnp.dot(x_zero, cross_v, preferred_element_type=jnp.float32).astype(jnp.bfloat16)
    scale = lax.dot_general(proj_b, cross_u, NT, preferred_element_type=jnp.float32) + cross_bias[None, :]
    x_float = x_zero.astype(jnp.float32)
    crossed = x_float * scale + x_float
    logit = jnp.sum(crossed * head[None, :], axis=1)
    delta = jax.nn.sigmoid(logit) - labels.astype(jnp.float32)
    upstream = delta[:, None] * head[None, :]
    dscale = upstream * x_float
    dscale_b = dscale.astype(jnp.bfloat16)
    dproj_b = jnp.dot(dscale_b, cross_u, preferred_element_type=jnp.float32).astype(jnp.bfloat16)

    pd_all = lax.all_gather(jnp.concatenate([proj_b, dproj_b], axis=1), AXES, axis=0, tiled=True)
    delta_all = lax.all_gather(delta, AXES, axis=0, tiled=True)

    part_u = lax.dot_general(dscale_b, proj_b, TN, preferred_element_type=jnp.float32)
    part_v = lax.dot_general(x_zero, dproj_b, TN, preferred_element_type=jnp.float32)
    part_c = jnp.sum(dscale, axis=0)
    share = depth // devices
    flat_c = jnp.pad(part_c.reshape(devices, 1, share), ((0, 0), (0, 7), (0, rank - share)))
    flat_c, pd_all, delta_all = lax.optimization_barrier((flat_c, pd_all, delta_all))
    parts = jnp.concatenate(
        [part_u.reshape(devices, share, rank), part_v.reshape(devices, share, rank), flat_c], axis=1
    )
    sums = lax.psum_scatter(parts, AXES, scatter_dimension=0, tiled=True)[0]

    pooled = upstream[:, width:] * (scale[:, width:] + 1.0) + lax.dot_general(
        dproj_b, cross_v[width:], NT, preferred_element_type=jnp.float32
    )
    pooled = pooled.astype(jnp.bfloat16).astype(jnp.float32)
    grads = pooled.reshape(samples, features, width).transpose(1, 0, 2).reshape(bags, width)
    hot_part = pl.pallas_call(
        functools.partial(hot_kernel, samples, features, lanes),
        out_shape=jax.ShapeDtypeStruct((hot_rows, width), jnp.bfloat16),
        in_specs=[pl.BlockSpec(memory_space=pltpu.SMEM), pl.BlockSpec(memory_space=pltpu.VMEM)],
        out_specs=pl.BlockSpec(memory_space=pltpu.VMEM),
        scratch_shapes=[pltpu.VMEM((hot_rows, width), jnp.float32)] * HOT_WAYS,
        compiler_params=pltpu.CompilerParams(vmem_limit_bytes=48 << 20),
        cost_estimate=pl.CostEstimate(flops=80_000_000_000, bytes_accessed=8 << 20, transcendentals=0),
        name="hot_sum",
    )(hot_ids.reshape(bags * lanes), grads)
    hot_part, sums = lax.optimization_barrier((hot_part, sums))
    hot_share = lax.psum_scatter(hot_part, AXES, scatter_dimension=0, tiled=True)
    hot_grad = lax.all_gather(hot_share, AXES, axis=0, tiled=True)

    c_rows = sums[2 * share:]
    c_high = c_rows.astype(jnp.bfloat16)
    c_left = c_rows - c_high.astype(jnp.float32)
    c_mid = c_left.astype(jnp.bfloat16)
    c_low = (c_left - c_mid.astype(jnp.float32)).astype(jnp.bfloat16)
    c_sent = jnp.concatenate([c_high[:1], c_mid[:1], c_low[:1], jnp.zeros_like(c_high[:5])], axis=0)
    sent = jnp.concatenate([sums[:2 * share].astype(jnp.bfloat16), c_sent], axis=0)
    sent, hot_grad = lax.optimization_barrier((sent, hot_grad))
    hot_grad = hot_grad.astype(jnp.float32)
    both = lax.all_gather(sent, AXES, axis=0, tiled=False)
    grad_u = both[:, :share].reshape(depth, rank)
    grad_v = both[:, share:2 * share].reshape(depth, rank)
    c_back = both[:, 2 * share:2 * share + 3, :share].astype(jnp.float32)
    sum_c = ((c_back[:, 0] + c_back[:, 1]) + c_back[:, 2]).reshape(depth)

    pair = 2 if features % 2 == 0 else 1
    pairs, wide = features // pair, pair * width
    whole = lambda i: (0, 0)
    whole3 = lambda i: (0, 0, 0)
    block = GROUP * samples
    cold_out = pl.pallas_call(
        functools.partial(cold_kernel, stride, row_bits),
        grid=(devices // GROUP,),
        out_shape=jax.ShapeDtypeStruct(cold_table.shape, jnp.float32),
        in_specs=[
            pl.BlockSpec((1, 1, GROUP * stride), lambda i: (i, 0, 0), memory_space=pltpu.SMEM),
            pl.BlockSpec((block, 2 * rank), lambda i: (i, 0)),
            pl.BlockSpec((block, 1), lambda i: (i, 0)),
            pl.BlockSpec((pairs, wide, rank), whole3),
            pl.BlockSpec((pairs, wide, rank), whole3),
            pl.BlockSpec((pairs, 1, wide), whole3),
            pl.BlockSpec((pairs, 1, wide), whole3),
            pl.BlockSpec((shard_rows, width), whole),
            pl.BlockSpec((shard_rows, 1), whole),
            pl.BlockSpec(memory_space=pl.ANY),
        ],
        out_specs=pl.BlockSpec((shard_rows, width), whole),
        scratch_shapes=[pltpu.VMEM((features * block, width), jnp.float32)]
        + [pltpu.VMEM((shard_rows + 8, width), jnp.float32)] * COLD_WAYS,
        compiler_params=pltpu.CompilerParams(vmem_limit_bytes=48 << 20),
        cost_estimate=pl.CostEstimate(flops=50_000_000_000, bytes_accessed=16 << 20, transcendentals=0),
        name="cold_sum",
    )(
        lists.reshape(devices // GROUP, 1, GROUP * stride),
        pd_all,
        delta_all[:, None],
        cross_u[width:].reshape(pairs, wide, rank),
        cross_v[width:].reshape(pairs, wide, rank),
        cross_bias[width:].reshape(pairs, 1, wide),
        head[width:].reshape(pairs, 1, wide),
        cold_table,
        cold_acc[:, None],
        hot_part,
    )

    new_acc = hot_acc + jnp.mean(hot_grad * hot_grad, axis=1)
    hot_out = hot_table - LEARN_RATE * hot_grad / (jnp.sqrt(new_acc)[:, None] + EPSILON)
    return (hot_out, cold_out, grad_u, grad_v, sum_c)


def solution(mesh):
    rows = P(AXES)
    placed = (rows, rows, P(), P(), P(), P(), P(), P(), rows, rows, rows, rows, rows)
    return jax.shard_map(
        per_device,
        mesh=mesh,
        in_specs=placed,
        out_specs=(P(), rows, P(), P(), P()),
        check_vma=False,
    )
```

time: 677 us -> 550 us (0.81); the launches traced: 669 us -> 549 us
  matrix products: 313 us -> 14.3 us
  waiting for transfers between devices: 0.04 us -> 220 us
  Pallas kernels: 0 us -> 182 us
  blocking collectives: 156 us -> 39.8 us
  local copies, waits for them, and re-layouts: 125 us -> 54.3 us
  other arithmetic: 46.6 us -> 14.5 us
    dot_general x16 -> x4, matrix products: 311 us -> 11.4 us  [the longest x1 4.32 us: per_device(): lax.dot_general(dproj_b, cross_v[width:], NT, preferred_element_type=jnp....]
    reduce_scatter x0 -> x2, waiting for transfers between devices: none -> 200 us  [the longest x1 136 us: per_device(): lax.psum_scatter(hot_part, AXES, scatter_dimension=0, tiled=True)]
    pallas_call x0 -> x3, Pallas kernels: none -> 182 us  [the longest x1 84.3 us: per_device(): pl.pallas_call(functools.partial(hot_kernel, samples, features, lanes), o...]
    psum x1 -> x0, blocking collectives: 156 us -> none  [per_device(): lax.psum((hot_local, part_u, part_v, part_c), ('wide', 'narrow'))]
    scatter x2 -> x0, local copies, waits for them, and re-layouts: 48.4 us -> none  [the longest x1 30.2 us: per_device(): jnp.zeros((devices * capacity, emb_width), jnp.bfloat16).at[target]]
    gather x4 -> x0, local copies, waits for them, and re-layouts: 41.1 us -> none  [the longest x1 19.9 us: per_device(): sorted_owner = owners[order]]
    optimization_barrier x0 -> x1, blocking collectives: none -> 39.8 us  [per_device(): lax.optimization_barrier((flat_c, pd_all, delta_all))]
    gather x4 -> x0, other arithmetic: 21.3 us -> none  [the longest x3 21.3 us: per_device(): position = jnp.arange(bag_count, dtype=jnp.int32) - starts[sorted_owner]]
  transfers between devices with their start and end apart: 3 -> 6, of which waited for: 0 -> 3; matrix products, arithmetic and copies ran while one was open for 49% -> 10% of each run, Pallas kernels for 0% -> 33%
where the time goes in v1:
time: 550 us; the launch traced here: 549 us
  waiting for transfers between devices  220 us (40%)
  Pallas kernels  182 us (33%)
  local copies, waits for them, and re-layouts  54.3 us (10%)
  blocking collectives  39.8 us (7%)
  other arithmetic  14.5 us (3%)
  matrix products  14.3 us (3%)
  between operations  14.1 us (3%)
  starting transfers between devices  9.52 us (2%)
    reduce_scatter x1, waiting for transfers between devices, per_device(): lax.psum_scatter(hot_part, AXES, scatter_dimension=0, tiled=True)  136 us
    pallas_call x1, Pallas kernels, per_device(): pl.pallas_call(functools.partial(hot_kernel, samples, features, lanes), o...  84.3 us
    pallas_call x1, Pallas kernels, per_device(): pl.pallas_call(functools.partial(cold_kernel, stride, row_bits), grid=(de...  76.4 us
    reduce_scatter x1, waiting for transfers between devices, per_device(): sums = lax.psum_scatter(parts, AXES, scatter_dimension=0, tiled=True)[0]  63.8 us
    optimization_barrier x1, blocking collectives, per_device(): lax.optimization_barrier((flat_c, pd_all, delta_all))  39.8 us
    pallas_call x1, Pallas kernels, per_device(): pl.pallas_call(functools.partial(list_kernel, samples, features, stride,...  21.6 us
    all_gather x1, waiting for transfers between devices, per_device(): hot_grad = lax.all_gather(hot_share, AXES, axis=0, tiled=True)  20.6 us
    reshape x2, local copies, waits for them, and re-layouts, per_device(): part_v.reshape(devices, share, rank)  15.2 us
  transfers between devices with their start and end apart: 6, of which 3 were waited for; matrix products, arithmetic and copies ran while one was open for 10% of the time, Pallas kernels for 33%

profile of v1, /device:TPU:24, one launch (start us, length us, event | category | flops | bytes accessed | tf_op | source)
XLA Modules:
  0.0 549.0 jit_solution(4748051703706344664)
XLA Ops:
  7.3 2.4 convolution_convert_fusion.1
  9.8 2.1 fusion.6
  15.0 2.4 convolution_bitcast_fusion
  17.5 10.0 %reshape.102 = f32[32,108,256]{1,0,2:T(8,128)} reshape(f32[3456,256]{0,1:T(8,128)} %convolution_bitcast_fusion) | data formatting | bytes 7077888 | tf_op jit(solution)/shard_map/reshape | solution.py:173
  27.4 5.2 copy.34
  32.6 2.5 fusion.10
  35.2 4.7 reshape.81
  39.8 39.8 %all-reduce.1 = f32[4608]{0:T(1024)} all-reduce(f32[4608]{0:T(1024)S(1)} %get-tuple-element.22), channel_id=1, replica_groups=mesh['wide'=8,'narrow'=4] {'wide','narrow'}, use_global_device_ids=true, to_apply=%add.1 | all-reduce | flops 4608 | bytes 36864 | tf_op jit(solution)/shard_map/optimization_barrier | solution.py:171
  79.6 5.4 pad_maximum_fusion
  86.1 3.3 copy.27
  89.4 2.7 reshape.77.ids_ref
  92.1 4.3 fusion.1
  99.2 84.3 %hot_sum.1.after_ref = bf16[8192,128]{1,0:T(8,128)(2,1)} custom-call(s32[71136]{0:T(1024)S(1)} %reshape.77.ids_ref, f32[3744,128]{1,0:T(8,128)S(1)} %bitcast.25), custom_call_target="tpu_custom_call" | custom-call | flops 80000000000 | bytes 8388608 | tf_op jit(solution)/shard_map/hot_sum/pallas_call | solution.py:182
  183.5 63.8 %reduce-scatter.3.cloned.1.call-done = f32[1,224,256]{2,1,0:T(8,128)} async-done(((f32[32,224,256]{2,1,0:T(8,128)}), f32[1,224,256]{2,1,0:T(8,128)}) %reduce-scatter.3.cloned.1.call-update) | async-done | bytes 229392 | tf_op jit(solution)/shard_map/reduce_scatter | solution.py:175
  247.6 135.8 %reduce-scatter.5.cloned.1.call-done = bf16[256,128]{1,0:T(8,128)(2,1)} async-done(((bf16[8192,128]{1,0:T(8,128)(2,1)}), bf16[256,128]{1,0:T(8,128)(2,1)}) %reduce-scatter.5.cloned.1.call-update) | async-done | bytes 65552 | tf_op jit(solution)/shard_map/reduce_scatter | solution.py:193
  385.1 21.6 %list_bags.1 = s32[16384]{0:T(1024)} custom-call(s32[3744]{0:T(1024)} %reshape.84.owner_ref, s32[3744]{0:T(1024)} %reshape.85.slot_ref, s32[1]{0:T(128)} %bitcast.4.me_ref), custom_call_target="tpu_custom_call" | custom-call | tf_op jit(solution)/shard_map/list_bags/pallas_call | solution.py:142
  406.8 9.1 %all-to-all-start = ((s32[32,1,512]{2,1,0:T(1,128)}), s32[32,1,512]{2,1,0:T(1,128)S(1)}, u32[]{:S(2)}, u32[]{:S(2)}) async-start(s32[32,1,512]{2,1,0:T(1,128)} %bitcast.32), calls=%async_computation.2 | async-start | bytes 131072 | tf_op jit(solution)/shard_map/all_to_all | solution.py:150
  420.4 3.0 broadcast_in_dim.17.delta_ref
  424.1 2.2 concatenate.11
  426.3 20.6 %all-gather.7.cloned.1.call-done = bf16[8192,128]{1,0:T(8,128)(2,1)} async-done(((bf16[256,128]{1,0:T(8,128)(2,1)}), bf16[8192,128]{1,0:T(8,128)(2,1)}) %all-gather.7.cloned.1.call-update) | async-done | bytes 2097168 | tf_op jit(solution)/shard_map/all_gather | solution.py:194
  449.4 76.4 %cold_sum.1 = f32[2048,128]{1,0:T(8,128)} custom-call(s32[8,1,2048]{2,1,0:T(1,128)S(1)} %bitcast.28, bf16[4608,512]{1,0:T(8,128)(2,1)} %all-gather.5.cloned.1.call-done.pd_ref, f32[4608,1]{1,0:T(8,128)} %broadcast_in_dim.17.delta_ref, bf16[13,256,256]{2,1,0:T(8,128)(2,1)S(1)} %bitcast.26, bf16[13,256,256]{2,1,0:T(8,128)(2,1)S(1)} %bitcast.27, ...), custom_call_target="tpu_custom_call" | custom-call | flops 49999998976 | bytes 16777216 | tf_op jit(solution)/shard_map/cold_sum/pallas_call | solution.py:216
  527.0 4.6 fusion.3
  531.6 4.3 fusion.18
  536.8 3.6 reshape.92
  (83 shorter events, 20.9 us)
Async XLA Ops:
  7.2 2.5 copy-start.2
  7.2 2.6 copy-start.5
  7.2 2.6 copy-start.9
  7.2 2.6 copy-start.12
  7.2 72.4 %all-gather.5.cloned.1.call-start = ((), (), s32[]{:S(2)}) async-start(), calls=%async_computation.3 | async-start | bytes 4866048 | tf_op jit(solution)/shard_map/all_gather | solution.py:163
  9.8 2.1 copy-start.18
  13.2 234.1 %reduce-scatter.3.cloned.1.call-start = ((), (), s32[]{:S(2)}) async-start(), calls=%async_computation.4 | async-start | bytes 7569408 | tf_op jit(solution)/shard_map/reduce_scatter | solution.py:175
  85.0 298.3 %reduce-scatter.5.cloned.1.call-start = ((), (), s32[]{:S(2)}) async-start(), calls=%async_computation.5 | async-start | bytes 2162688 | tf_op jit(solution)/shard_map/reduce_scatter | solution.py:193
  89.4 2.7 copy-start.3
  183.5 199.9 %copy-start.16 = (s32[144,26,1]{0,2,1:T(1,128)S(1)}, s32[144,26,1]{0,2,1:T(1,128)}, u32[]{:S(2)}) copy-start(s32[144,26,1]{0,2,1:T(1,128)} %param.24) | copy-start | bytes 44932
  183.5 200.7 %copy-start.15 = (s32[144,26]{0,1:T(8,128)S(1)}, s32[144,26]{0,1:T(8,128)}, u32[]{:S(2)}) copy-start(s32[144,26]{0,1:T(8,128)} %param.25) | copy-start | bytes 44932
  183.5 232.4 %copy-start.6 = (bf16[3456,256]{1,0:T(8,128)(2,1)S(1)}, bf16[3456,256]{1,0:T(8,128)(2,1)}, u32[]{:S(2)}) copy-start(bf16[3456,256]{1,0:T(8,128)(2,1)} %param.15) | copy-start | bytes 5308420
  247.3 199.6 %all-gather.7.cloned.1.call-start = ((), (), s32[]{:S(2)}) async-start(), calls=%async_computation.6 | async-start | bytes 2162688 | tf_op jit(solution)/shard_map/all_gather | solution.py:194
  406.8 40.2 %all-to-all-start = ((s32[32,1,512]{2,1,0:T(1,128)}), s32[32,1,512]{2,1,0:T(1,128)S(1)}, u32[]{:S(2)}, u32[]{:S(2)}) async-start(s32[32,1,512]{2,1,0:T(1,128)} %bitcast.32), calls=%async_computation.2 | async-start | bytes 131072 | tf_op jit(solution)/shard_map/all_to_all | solution.py:150
  415.9 115.7 %all-gather.9.cloned.1.call-start = ((), (), s32[]{:S(2)}) async-start(), calls=%async_computation.7 | async-start | bytes 3784704 | tf_op jit(solution)/shard_map/all_gather | solution.py:205
  416.1 1.6 copy-start.13
  416.1 3.0 copy-start.17
  416.1 4.3 copy-start.10
  420.4 3.0 copy-start.11
  446.9 1.2 copy-start
  448.2 1.2 copy-start.1
  449.4 76.4 %copy-start.4 = (bf16[8192,128]{1,0:T(8,128)(2,1)S(1)}, bf16[8192,128]{1,0:T(8,128)(2,1)}, u32[]{:S(2)}) copy-start(bf16[8192,128]{1,0:T(8,128)(2,1)} %all-gather.7.cloned.1.call-done) | copy-start | bytes 6291460
  449.4 77.6 %copy-start.7 = (f32[8192,128]{1,0:T(8,128)S(1)}, f32[8192,128]{1,0:T(8,128)}, u32[]{:S(2)}) copy-start(f32[8192,128]{1,0:T(8,128)} %param.19) | copy-start | bytes 12582916
  525.8 1.2 copy-start.14
  (1 other events, 1.1 us)
Sparse Core Ops, SparseCore 0:
  13.3 63.5 all-gather.4
  85.2 162.1 reduce-scatter.2
  249.6 133.7 reduce-scatter.4
  386.6 60.2 all-gather.6
  450.6 59.3 all-gather.8
